TPU v7x, 256 devices: a whole 4x4x8 slice. The times are simulated.
256 devices in a mesh: row: 16 (over z, y_hi), col: 16 (over y_lo, x, core).
Axes of the slice: x: 4, y: 4 (y_hi: 2, y_lo: 2; y = y_hi * 2 + y_lo), z: 8, core: 2. Of those that a mesh axis runs over, the one named last changes fastest.
Arguments:
- queries: bfloat16 [65536, 768], P(('row', 'col')), may hold values from -20 to 20
- keys: bfloat16 [65536, 768], P(('row', 'col')), may hold values from -20 to 20
- values: bfloat16 [65536, 768], P(('row', 'col')), may hold values from -6 to 6
- grad_out: bfloat16 [65536, 768], P(('row', 'col')), may hold values from -96 to 96
Outputs:
- grad_queries: bfloat16 [65536, 768], P(('row', 'col'))
- grad_keys: bfloat16 [65536, 768], P(('row', 'col'))
- grad_values: bfloat16 [65536, 768], P(('row', 'col'))
All inputs are finite; a program needn't handle non-finite values.
Results may differ from a plain program's by a relative error of at most 0.0097.
Values may be sent and summed in bfloat16 or wider, within the bound.
A program may use at most 128 MiB of HBM per device.

v0:
```python
import jax
import jax.numpy as jnp
from jax import lax
from jax.experimental import pallas as pl
from jax.experimental.pallas import tpu as pltpu
from jax.sharding import PartitionSpec as P

HEADS = 12
HEAD_DIM = 64
TOK = 256
WIDTH = 768
LANES = 128
SCALE = HEAD_DIM**-0.5
NEG_FILL = -1e30
PAIRS = HEADS // 2
MESH = pl.DeviceIdType.MESH
F32 = jnp.float32
BF16 = jnp.bfloat16


def mm(a, b):
    return lax.dot_general(a, b, (((1,), (0,)), ((), ())), preferred_element_type=F32)


def mm_nt(a, b):
    return lax.dot_general(a, b, (((1,), (1,)), ((), ())), preferred_element_type=F32)


def mm_tn(a, b):
    return lax.dot_general(a, b, (((0,), (0,)), ((), ())), preferred_element_type=F32)


def iota(shape, dim):
    return lax.broadcasted_iota(jnp.int32, shape, dim)


def onehot(hit, value=1.0):
    return jnp.where(hit, value, 0.0).astype(BF16)


def move(rows, table):
    high = rows.astype(BF16)
    rest = rows - high.astype(F32)
    middle = rest.astype(BF16)
    low = (rest - middle.astype(F32)).astype(BF16)
    return mm(high, table) + mm(middle, table) + mm(low, table)


def swap(tile):
    return pltpu.roll(tile, HEAD_DIM, 1)


def reversed_digits(index):
    return (index & 3) * 64 + ((index >> 2) & 3) * 16 + ((index >> 4) & 3) * 4 + (index >> 6)


def forward(scores, dprob):
    row_max = jnp.max(scores, axis=0, keepdims=True)
    weights = jnp.exp(scores - row_max)
    row_sum = jnp.sum(weights, axis=0, keepdims=True)
    dot_sum = jnp.sum(weights * dprob, axis=0, keepdims=True)
    return weights, stat_tile(row_max + jnp.log(row_sum), dot_sum / row_sum, row_max)


def stat_tile(lse, delta, row_max):
    row = iota((8, TOK), 0)
    return jnp.where(row == 0, lse, jnp.where(row == 1, delta, jnp.where(row == 2, row_max, 0.0)))


def backward(weights, dprob, row_max, lse, delta):
    probs = weights * jnp.exp(row_max - lse)
    dscore = probs * (dprob - delta)
    return probs.astype(BF16), dscore.astype(BF16)


def merge(parts):
    top = parts[0][0]
    for lse, _ in parts[1:]:
        top = jnp.maximum(top, lse)
    norm = 0.0
    total = 0.0
    for lse, delta in parts:
        factor = jnp.exp(lse - top)
        norm = norm + factor
        total = total + factor * delta
    return top + jnp.log(norm), total / norm


def rows_of(tile):
    return tile[0:1], tile[1:2]


def masked_rows(tile, hit):
    lse, delta = rows_of(tile)
    return jnp.where(hit, lse, NEG_FILL), jnp.where(hit, delta, 0.0)


def kernel(
    q_ref, k_ref, v_ref, g_ref, dq_ref, dk_ref, dv_ref,
    qp, kp, vp, gp, acc_q, acc_k, acc_v,
    w_all, d_all, pack, recv_a, recv_l, sel_c, sel_d,
    st1, st2, st_l, fin1, fin2, fin_l, st3,
    a_own, b_own, c_two, d_two, e_four, f_five, g_three, h_three, i_three, j_three,
    out2, out_l, back4, back5, back2, back3,
    send_sem, recv_sem,
):
    row = lax.axis_index("row")
    col = lax.axis_index("col")
    member = lax.rem(col, 4)
    group = col // 4
    row_in = lax.rem(row, 4)
    row_group = row // 4
    is3 = col < HEADS
    is4 = jnp.logical_and(col >= HEADS, row_in < 3)
    is5 = jnp.logical_and(jnp.logical_and(col >= HEADS, row_in == 3), row_group < 3)
    has_long = jnp.logical_or(is3, jnp.logical_or(is4, is5))
    is45 = jnp.logical_or(is4, is5)
    row4, col4 = row_group * 4 + group, HEADS + member
    row5 = group * 4 + 3
    head4 = row_in * 4 + (col - HEADS)
    head5 = row_group * 4 + (col - HEADS)
    col_of4 = jnp.where(is4, head4, 0)
    col_of5 = jnp.where(is5, head5, 0)

    sends = []

    def post(src, dst, recv, to_row, to_col, cond=None, maybe_self=False):
        slot = len(sends)
        copy = pltpu.make_async_remote_copy(
            src_ref=src, dst_ref=dst, send_sem=send_sem.at[slot], recv_sem=recv_sem.at[recv],
            device_id=(to_row, to_col), device_id_type=MESH,
        )
        away = cond
        if maybe_self:
            same = jnp.logical_and(to_col == col, to_row == row)
            other = jnp.logical_not(same)
            away = other if cond is None else jnp.logical_and(cond, other)
            here = same if cond is None else jnp.logical_and(cond, same)

            @pl.when(here)
            def _():
                pltpu.make_async_copy(src, dst, recv_sem.at[recv]).start()

        if away is None:
            copy.start()
        else:
            pl.when(away)(copy.start)
        sends.append((away, copy))

    def arrive(buffer, recv):
        pltpu.make_async_copy(buffer, buffer, recv_sem.at[recv]).wait()

    barrier = pltpu.get_barrier_semaphore()

    def greet(to_row, to_col):
        pl.semaphore_signal(barrier, inc=1, device_id=(to_row, to_col), device_id_type=MESH)

    for apart in range(1, 16):
        greet(row, lax.rem(col + apart, 16))

    @pl.when(is3)
    def _():
        greet(row4, col4)
        greet(row5, col4)

    @pl.when(is4)
    def _():
        for step in range(4):
            greet(row_group * 4 + step, col_of4)

    @pl.when(is5)
    def _():
        for step in range(16):
            greet(step, col_of5)

    order = reversed_digits(iota((TOK, TOK), 0)) == iota((TOK, TOK), 1)
    permute = onehot(order)
    permute_scaled = onehot(order, SCALE)
    qp[...] = mm(permute_scaled, q_ref[...]).astype(BF16)
    kp[...] = mm(permute, k_ref[...]).astype(BF16)
    vp[...] = mm(permute, v_ref[...]).astype(BF16)
    gp[...] = mm(permute, g_ref[...]).astype(BF16)

    low64 = iota((64, LANES), 1) < HEAD_DIM
    low256 = iota((TOK, LANES), 1) < HEAD_DIM

    for w in range(4):
        rows = slice(64 * w, 64 * w + 64)
        for i in range(3):
            tile = slice(LANES * (2 * i + w // 2), LANES * (2 * i + w // 2) + LANES)
            for slot, (first, second) in enumerate(((qp, gp), (kp, vp))):
                one = first[rows, tile].astype(F32)
                two = second[rows, tile].astype(F32)
                if w % 2 == 0:
                    two = swap(two)
                else:
                    one = swap(one)
                pack[w, i, slot] = jnp.where(low64, one, two).astype(BF16)

    pl.semaphore_wait(barrier, 15 + jnp.where(is3, 2, jnp.where(is4, 4, jnp.where(is5, 16, 0))))

    for h in range(HEADS):
        w, i = h % 4, h // 4
        post(
            pack.at[w, i, :, pl.ds(16 * i, 16), :],
            recv_l.at[:, pl.ds(pl.multiple_of(16 * col, 16), 16), :],
            1, row, h, maybe_self=True,
        )
    my_rows = pl.ds(pl.multiple_of(64 * member, 64), 64)
    for apart in (2, 3, 1):
        w = lax.rem(member + apart, 4)
        post(pack.at[w], recv_a.at[:, :, my_rows, :], 0, row, group * 4 + w)
    pltpu.make_async_copy(pack.at[member], recv_a.at[:, :, my_rows, :], recv_sem.at[0]).start()

    def pair_forward(j, carry):
        lanes = pl.ds(pl.multiple_of(j * LANES, LANES), LANES)
        q, k, v, g = qp[:, lanes], kp[:, lanes], vp[:, lanes], gp[:, lanes]
        zero = jnp.zeros_like(k)
        i = j // 2
        for parity in range(2):
            mine = low256 if parity == 0 else jnp.logical_not(low256)
            scores = mm_nt(jnp.where(mine, k, zero), q)
            dprob = mm_nt(jnp.where(mine, v, zero), g)
            weights, stat = forward(scores, dprob)
            w_all[2 * j + parity] = weights
            d_all[2 * j + parity] = dprob
            st1[2 * lax.rem(j, 2) + parity, i] = stat
        return carry

    def packed_forward(query_side, key_side, unit):
        zero = jnp.zeros_like(key_side)
        scores = mm_nt(jnp.where(low256, key_side, zero), query_side)
        dprob = mm_nt(jnp.where(low256, zero, key_side), query_side)
        weights, stat = forward(scores, dprob)
        w_all[unit] = weights
        d_all[unit] = dprob
        return stat

    lax.fori_loop(0, 3, pair_forward, 0)

    @pl.when(is3)
    def _():
        arrive(recv_l, 1)
        pick4 = onehot(
            iota((64, TOK), 1) == 16 * (iota((64, TOK), 0) >> 2) + (iota((64, TOK), 0) & 3)
        )
        pick5 = onehot(iota((16, TOK), 1) == 16 * iota((16, TOK), 0))
        for slot in range(2):
            sel_c[slot] = mm(pick4, recv_l[slot]).astype(BF16)
            sel_d[slot] = mm(pick5, recv_l[slot]).astype(BF16)

    post(sel_c, recv_l.at[:, pl.ds(pl.multiple_of(64 * row_in, 64), 64), :], 1, row4, col4, cond=is3)
    post(sel_d, recv_l.at[:, pl.ds(pl.multiple_of(16 * row, 16), 16), :], 1, row5, col4, cond=is3)

    lax.fori_loop(3, PAIRS, pair_forward, 0)

    for h in range(HEADS):
        w, i = h % 4, h // 4
        post(
            st1.at[w, i, :, pl.ds(LANES * (w // 2), LANES)], a_own.at[col], 2, row, h,
            maybe_self=True,
        )
    for apart in range(4):
        w = lax.rem(member + apart, 4)
        post(
            st1.at[w, :, :, pl.ds(pl.multiple_of(LANES * (w // 2), LANES), LANES)],
            b_own.at[member], 3, row, group * 4 + w, maybe_self=True,
        )

    arrive(recv_a, 0)
    for i in range(3):
        st2[i] = packed_forward(recv_a[i, 0], recv_a[i, 1], HEADS + i)
    for i in range(3):
        post(st2.at[i], d_two.at[group], 5, row, member + 4 * i, maybe_self=True)
    for apart in range(4):
        w = lax.rem(member + apart, 4)
        post(
            st2.at[:, :, pl.ds(pl.multiple_of(LANES * (w // 2), LANES), LANES)],
            c_two.at[member], 4, row, group * 4 + w, maybe_self=True,
        )

    @pl.when(is45)
    def _():
        arrive(recv_l, 1)

    @pl.when(has_long)
    def _():
        st_l[...] = packed_forward(recv_l[0], recv_l[1], HEADS + 3)

    for step in range(4):
        post(
            st_l.at[:, pl.ds(LANES * (step // 2), LANES)], e_four, 6,
            row_group * 4 + step, col_of4, cond=is4,
        )
    for step in range(16):
        post(
            st_l.at[:, pl.ds(LANES * (step // 8), LANES)], f_five, 7, step, col_of5, cond=is5
        )

    lane = iota((1, TOK), 1)
    src128 = iota((LANES, TOK), 0)
    dst128 = iota((LANES, TOK), 1)
    src256 = iota((TOK, TOK), 0)
    dst256 = iota((TOK, TOK), 1)

    def picked(moved, count, hit):
        total = jnp.zeros((8, TOK), F32)
        for step in range(count):
            total = total + jnp.where(hit(step), moved[step], 0.0)
        return total

    @pl.when(is3)
    def _():
        arrive(a_own, 2)
        start = 64 * lax.rem(member, 2) + 16 * group
        one = move(
            a_own[...].reshape(16 * 8, LANES), onehot(src128 == start + (dst128 & 15))
        ).reshape(16, 8, TOK)
        one = rows_of(picked(one, 16, lambda c: (lane >> 4) == c))
        arrive(d_two, 5)
        two = move(
            d_two[...].reshape(4 * 8, TOK),
            onehot(src256 == 64 * ((dst256 >> 4) & 3) + 16 * group + (dst256 & 15)),
        ).reshape(4, 8, TOK)
        two = rows_of(picked(two, 4, lambda c: (lane >> 6) == c))
        arrive(e_four, 6)
        four = move(
            e_four[...],
            onehot(
                jnp.logical_and(
                    src128 == 64 * lax.rem(row_in, 2) + 4 * (dst128 >> 4) + (dst128 & 15),
                    (dst128 & 15) < 4,
                )
            ),
        )
        four = masked_rows(four, (lane & 15) < 4)
        arrive(f_five, 7)
        five = move(
            f_five[...],
            onehot(
                jnp.logical_and(
                    src128 == 16 * lax.rem(row, 8) + (dst128 >> 4), (dst128 & 15) == 0
                )
            ),
        )
        five = masked_rows(five, (lane & 15) == 0)
        lse, delta = merge([one, two, rows_of(st_l[...]), four, five])
        st3[...] = stat_tile(lse, delta, 0.0)
        fin_l[...] = stat_tile(lse, delta, 0.0)

    post(st3, i_three.at[row_in], 10, row4, col4, cond=is3)
    post(st3, j_three.at[row], 11, row5, col4, cond=is3)
    col_head = jnp.where(is3, col, 0)
    for step in range(4):
        post(
            st3.at[:, pl.ds(LANES * (step // 2), LANES)], h_three.at[jnp.where(is3, group, 0)], 9,
            row, step * 4 + member, cond=is3, maybe_self=True,
        )
    for step in range(16):
        post(
            st3.at[:, pl.ds(LANES * (step // 8), LANES)], g_three.at[col_head], 8,
            row, step, cond=is3, maybe_self=True,
        )

    @pl.when(is4)
    def _():
        arrive(i_three, 10)
        total = move(
            i_three[...].reshape(4 * 8, TOK),
            onehot(src256 == 16 * ((dst256 >> 2) & 15) + (dst256 & 3)),
        ).reshape(4, 8, TOK)
        fin_l[...] = picked(total, 4, lambda c: (lane >> 6) == c)

    @pl.when(is5)
    def _():
        arrive(j_three, 11)
        total = move(
            j_three[...].reshape(16 * 8, TOK), onehot(src256 == 16 * (dst256 & 15))
        ).reshape(16, 8, TOK)
        fin_l[...] = picked(total, 16, lambda c: (lane >> 4) == c)

    def packed_backward(query_side, key_side, unit, stat, final):
        probs, dscore = backward(
            w_all[unit], d_all[unit], stat[2:3], final[0:1], final[1:2]
        )
        zero = jnp.zeros_like(key_side)
        both = mm(dscore, jnp.where(low256, query_side, zero)) + mm(
            probs, jnp.where(low256, zero, query_side)
        )
        return both, mm_tn(dscore, jnp.where(low256, key_side, zero))

    @pl.when(has_long)
    def _():
        both, own = packed_backward(recv_l[0], recv_l[1], HEADS + 3, st_l[...], fin_l[...])
        out_l[0] = both.astype(BF16)
        out_l[1] = own.astype(BF16)

    for step in range(4):
        post(
            out_l.at[:, pl.ds(64 * step, 64), :], back4, 12,
            row_group * 4 + step, col_of4, cond=is4,
        )
    for step in range(16):
        post(out_l.at[:, pl.ds(16 * step, 16), :], back5, 13, step, col_of5, cond=is5)

    spread64 = onehot(src128 == 64 * lax.rem(member, 2) + (dst128 & 63))
    arrive(b_own, 3)
    arrive(h_three, 9)
    own2 = move(b_own[...].reshape(4 * 3 * 8, LANES), spread64).reshape(4, 3, 8, TOK)
    long2 = move(
        h_three[...].reshape(3 * 8, LANES),
        onehot(src128 == 64 * lax.rem(group, 2) + 16 * (dst128 >> 6) + (dst128 & 15)),
    ).reshape(3, 8, TOK)
    for i in range(3):
        one = rows_of(picked(own2[:, i], 4, lambda c: (lane >> 6) == c))
        lse, delta = merge([one, rows_of(st2[i])])
        long = ((lane >> 4) & 3) == i
        fin2[i] = stat_tile(
            jnp.where(long, long2[i][0:1], lse), jnp.where(long, long2[i][1:2], delta), 0.0
        )

    def two_backward(i, carry):
        both, own = packed_backward(recv_a[i, 0], recv_a[i, 1], HEADS + i, st2[i], fin2[i])
        out2[i, 0] = both.astype(BF16)
        out2[i, 1] = own.astype(BF16)
        return carry

    lax.fori_loop(0, 3, two_backward, 0)
    for apart in range(4):
        w = lax.rem(member + apart, 4)
        post(
            out2.at[:, :, pl.ds(pl.multiple_of(64 * w, 64), 64), :],
            back2.at[member], 14, row, group * 4 + w, maybe_self=True,
        )

    @pl.when(is3)
    def _():
        place4 = onehot(
            iota((TOK, 64), 0) == 16 * (iota((TOK, 64), 1) >> 2) + (iota((TOK, 64), 1) & 3)
        )
        place5 = onehot(iota((TOK, 16), 0) == 16 * iota((TOK, 16), 1))
        arrive(back4, 12)
        arrive(back5, 13)
        for slot in range(2):
            total = out_l[slot].astype(F32) + mm(place4, back4[slot]) + mm(place5, back5[slot])
            out_l[slot] = total.astype(BF16)

    for step in range(16):
        post(
            out_l.at[:, pl.ds(16 * step, 16), :], back3.at[col_head], 15,
            row, step, cond=is3, maybe_self=True,
        )

    arrive(c_two, 4)
    arrive(g_three, 8)
    two1 = move(c_two[...].reshape(HEADS * 8, LANES), spread64).reshape(4, 3, 8, TOK)
    three1 = move(
        g_three[...].reshape(HEADS * 8, LANES),
        onehot(src128 == 16 * lax.rem(col, 8) + (dst128 & 15)),
    ).reshape(HEADS, 8, TOK)
    for h in range(HEADS):
        w, i = h % 4, h // 4
        one = rows_of(st1[w, i])
        lse, delta = merge([one, masked_rows(two1[w, i], (lane >> 6) == w)])
        long = (lane >> 4) == 4 * w + i
        fin1[h] = stat_tile(
            jnp.where(long, three1[h][0:1], lse), jnp.where(long, three1[h][1:2], delta), 0.0
        )

    def pair_backward(j, carry):
        lanes = pl.ds(pl.multiple_of(j * LANES, LANES), LANES)
        q, k, g = qp[:, lanes], kp[:, lanes], gp[:, lanes]
        zero = jnp.zeros_like(k)
        i = j // 2
        sum_q = sum_k = sum_v = 0.0
        for parity in range(2):
            mine = low256 if parity == 0 else jnp.logical_not(low256)
            h = 2 * j + parity
            stat = st1[2 * lax.rem(j, 2) + parity, i]
            final = fin1[h]
            probs, dscore = backward(w_all[h], d_all[h], stat[2:3], final[0:1], final[1:2])
            sum_v = sum_v + mm(probs, jnp.where(mine, g, zero))
            sum_k = sum_k + mm(dscore, jnp.where(mine, q, zero))
            sum_q = sum_q + mm_tn(dscore, jnp.where(mine, k, zero))
        acc_q[:, lanes] = sum_q
        acc_k[:, lanes] = sum_k
        acc_v[:, lanes] = sum_v
        return carry

    lax.fori_loop(0, PAIRS, pair_backward, 0)

    arrive(back2, 14)
    arrive(back3, 15)
    for h in range(HEADS):
        w, i = h % 4, h // 4
        tile = slice(LANES * (2 * i + w // 2), LANES * (2 * i + w // 2) + LANES)
        for count, start, both, own in (
            (64, 64 * w, back2[w, i, 0], back2[w, i, 1]),
            (16, 64 * w + 16 * i, back3[h, 0], back3[h, 1]),
        ):
            rows = slice(start, start + count)
            low = iota((count, LANES), 1) < HEAD_DIM
            both = both.astype(F32)
            own = own.astype(F32)
            other = swap(both)
            if w % 2 == 0:
                grad_k = jnp.where(low, both, 0.0)
                grad_v = jnp.where(low, other, 0.0)
            else:
                grad_k = jnp.where(low, 0.0, other)
                grad_v = jnp.where(low, 0.0, both)
                own = swap(own)
            acc_q[rows, tile] += own
            acc_k[rows, tile] += grad_k
            acc_v[rows, tile] += grad_v
    dq_ref[...] = mm(permute_scaled, acc_q[...].astype(BF16)).astype(BF16)
    dk_ref[...] = mm(permute, acc_k[...].astype(BF16)).astype(BF16)
    dv_ref[...] = mm(permute, acc_v[...].astype(BF16)).astype(BF16)

    for away, copy in sends:
        if away is None:
            copy.wait_send()
        else:
            pl.when(away)(copy.wait_send)


def body(queries, keys, values, grad_out):
    def vm(shape, kind):
        return pltpu.VMEM(shape, kind)

    whole = pl.BlockSpec(memory_space=pltpu.VMEM)
    return pl.pallas_call(
        kernel,
        out_shape=[jax.ShapeDtypeStruct((TOK, WIDTH), BF16)] * 3,
        in_specs=[whole] * 4,
        out_specs=[whole] * 3,
        scratch_shapes=[vm((TOK, WIDTH), BF16)] * 4
        + [vm((TOK, WIDTH), F32)] * 3
        + [
            vm((16, TOK, TOK), F32),
            vm((16, TOK, TOK), F32),
            vm((4, 3, 2, 64, LANES), BF16),
            vm((3, 2, TOK, LANES), BF16),
            vm((2, TOK, LANES), BF16),
            vm((2, 64, LANES), BF16),
            vm((2, 16, LANES), BF16),
            vm((4, 3, 8, TOK), F32),
            vm((3, 8, TOK), F32),
            vm((8, TOK), F32),
            vm((HEADS, 8, TOK), F32),
            vm((3, 8, TOK), F32),
            vm((8, TOK), F32),
            vm((8, TOK), F32),
            vm((16, 8, LANES), F32),
            vm((4, 3, 8, LANES), F32),
            vm((4, 3, 8, LANES), F32),
            vm((4, 8, TOK), F32),
            vm((8, LANES), F32),
            vm((8, LANES), F32),
            vm((HEADS, 8, LANES), F32),
            vm((3, 8, LANES), F32),
            vm((4, 8, TOK), F32),
            vm((16, 8, TOK), F32),
            vm((3, 2, TOK, LANES), BF16),
            vm((2, TOK, LANES), BF16),
            vm((2, 64, LANES), BF16),
            vm((2, 16, LANES), BF16),
            vm((4, 3, 2, 64, LANES), BF16),
            vm((HEADS, 2, 16, LANES), BF16),
            pltpu.SemaphoreType.DMA((128,)),
            pltpu.SemaphoreType.DMA((16,)),
        ],
        compiler_params=pltpu.CompilerParams(
            collective_id=0, has_side_effects=True, vmem_limit_bytes=48 * 1024 * 1024
        ),
    )(queries, keys, values, grad_out)


def solution(mesh):
    spec = P(("row", "col"), None)
    return jax.shard_map(
        body, mesh=mesh, in_specs=(spec,) * 4, out_specs=(spec,) * 3, check_vma=False
    )
```

profile of v0, /device:TPU:1, one launch (start us, length us, event | category | flops | bytes accessed | tf_op | source)
XLA Modules:
  0.0 57.6 jit_solution(16100078639927869627)
XLA Ops:
  0.6 0.0 copy-start
  0.6 1.0 %copy-done = bf16[256,768]{1,0:T(8,128)(2,1)S(1)} copy-done((bf16[256,768]{1,0:T(8,128)(2,1)S(1)}, bf16[256,768]{1,0:T(8,128)(2,1)}, u32[]{:S(2)}) %copy-start) | copy-done | bytes 393240
  1.6 0.0 copy-start.1
  1.6 1.0 %copy-done.1 = bf16[256,768]{1,0:T(8,128)(2,1)S(1)} copy-done((bf16[256,768]{1,0:T(8,128)(2,1)S(1)}, bf16[256,768]{1,0:T(8,128)(2,1)}, u32[]{:S(2)}) %copy-start.1) | copy-done | bytes 393240
  2.6 0.0 copy-start.2
  2.6 1.0 %copy-done.2 = bf16[256,768]{1,0:T(8,128)(2,1)S(1)} copy-done((bf16[256,768]{1,0:T(8,128)(2,1)S(1)}, bf16[256,768]{1,0:T(8,128)(2,1)}, u32[]{:S(2)}) %copy-start.2) | copy-done | bytes 393240
  3.6 0.0 copy-start.3
  3.6 1.0 %copy-done.3 = bf16[256,768]{1,0:T(8,128)(2,1)S(1)} copy-done((bf16[256,768]{1,0:T(8,128)(2,1)S(1)}, bf16[256,768]{1,0:T(8,128)(2,1)}, u32[]{:S(2)}) %copy-start.3) | copy-done | bytes 393240
  4.6 50.7 %shard_map.67 = (bf16[256,768]{1,0:T(8,128)(2,1)S(1)}, bf16[256,768]{1,0:T(8,128)(2,1)S(1)}, bf16[256,768]{1,0:T(8,128)(2,1)S(1)}) custom-call(bf16[256,768]{1,0:T(8,128)(2,1)S(1)} %copy-done, bf16[256,768]{1,0:T(8,128)(2,1)S(1)} %copy-done.1, bf16[256,768]{1,0:T(8,128)(2,1)S(1)} %copy-done.2, bf16[256,768]{1,0:T(8,128)(2,1)S(1)} %copy-done.3), custom_call_target="tpu_custom_call" | custom-call | tf_op jit(solution)/shard_map/pallas_call | solution.py:532
  55.3 0.7 %copy.10 = bf16[256,768]{1,0:T(8,128)(2,1)} copy(bf16[256,768]{1,0:T(8,128)(2,1)S(1)} %get-tuple-element.6) | data formatting | bytes 786432
  56.1 0.7 %copy.11 = bf16[256,768]{1,0:T(8,128)(2,1)} copy(bf16[256,768]{1,0:T(8,128)(2,1)S(1)} %get-tuple-element.7) | data formatting | bytes 786432
  56.8 0.7 %copy.12 = bf16[256,768]{1,0:T(8,128)(2,1)} copy(bf16[256,768]{1,0:T(8,128)(2,1)S(1)} %get-tuple-element.8) | data formatting | bytes 786432
Async XLA Ops:
  0.6 1.0 %copy-start = (bf16[256,768]{1,0:T(8,128)(2,1)S(1)}, bf16[256,768]{1,0:T(8,128)(2,1)}, u32[]{:S(2)}) copy-start(bf16[256,768]{1,0:T(8,128)(2,1)} %q_ref.1) | copy-start | bytes 1179652
  1.6 1.0 %copy-start.1 = (bf16[256,768]{1,0:T(8,128)(2,1)S(1)}, bf16[256,768]{1,0:T(8,128)(2,1)}, u32[]{:S(2)}) copy-start(bf16[256,768]{1,0:T(8,128)(2,1)} %k_ref.1) | copy-start | bytes 1179652
  2.6 1.0 %copy-start.2 = (bf16[256,768]{1,0:T(8,128)(2,1)S(1)}, bf16[256,768]{1,0:T(8,128)(2,1)}, u32[]{:S(2)}) copy-start(bf16[256,768]{1,0:T(8,128)(2,1)} %v_ref.1) | copy-start | bytes 1179652
  3.6 1.0 %copy-start.3 = (bf16[256,768]{1,0:T(8,128)(2,1)S(1)}, bf16[256,768]{1,0:T(8,128)(2,1)}, u32[]{:S(2)}) copy-start(bf16[256,768]{1,0:T(8,128)(2,1)} %g_ref.1) | copy-start | bytes 1179652
where the time goes:
time: 57.8 us; the launch traced here: 57.6 us
  Pallas kernels  50.7 us (88%)
  local copies, waits for them, and re-layouts  6.21 us (11%)
  between operations  0.65 us (1%)
    pallas_call x1, Pallas kernels, body(): pl.pallas_call(kernel, out_shape=[jax.ShapeDtypeStruct((TOK, WIDTH), BF16...  50.7 us
    unnamed x11, local copies, waits for them, and re-layouts  6.21 us

commit v1 on v0

--- a/solution.py
+++ b/solution.py
@@ -96,13 +96,13 @@
 
 
 def kernel(
-    q_ref, k_ref, v_ref, g_ref, dq_ref, dk_ref, dv_ref,
-    qp, kp, vp, gp, acc_q, acc_k, acc_v,
-    w_all, d_all, pack, recv_a, recv_l, sel_c, sel_d,
-    st1, st2, st_l, fin1, fin2, fin_l, st3,
-    a_own, b_own, c_two, d_two, e_four, f_five, g_three, h_three, i_three, j_three,
-    out2, out_l, back4, back5, back2, back3,
-    send_sem, recv_sem,
+    q_hbm, k_hbm, v_hbm, g_hbm, sum_q, sum_k, sum_v,
+    q_in, k_in, v_in, g_in, qp, kp, vp, gp, acc_q, acc_k, acc_v,
+    w_all, d_all, pack, recv_a, recv3, recv4, recv5, sel4, sel5,
+    st1, st2, st_l, fin1, fin2, st3,
+    a_own, b_own, c_two, d_two, g_three, h_three, i_three, j_three,
+    out2, out_l, part4, part5, back2, back3,
+    send_sem, recv_sem, load_sem,
 ):
     row = lax.axis_index("row")
     col = lax.axis_index("col")
@@ -111,16 +111,14 @@
     row_in = lax.rem(row, 4)
     row_group = row // 4
     is3 = col < HEADS
-    is4 = jnp.logical_and(col >= HEADS, row_in < 3)
-    is5 = jnp.logical_and(jnp.logical_and(col >= HEADS, row_in == 3), row_group < 3)
-    has_long = jnp.logical_or(is3, jnp.logical_or(is4, is5))
-    is45 = jnp.logical_or(is4, is5)
-    row4, col4 = row_group * 4 + group, HEADS + member
-    row5 = group * 4 + 3
-    head4 = row_in * 4 + (col - HEADS)
-    head5 = row_group * 4 + (col - HEADS)
-    col_of4 = jnp.where(is4, head4, 0)
-    col_of5 = jnp.where(is5, head5, 0)
+
+    loads = []
+    for slot, (src, dst) in enumerate(
+        ((q_hbm, q_in), (g_hbm, g_in), (k_hbm, k_in), (v_hbm, v_in))
+    ):
+        load = pltpu.make_async_copy(src, dst, load_sem.at[slot])
+        load.start()
+        loads.append(load)
 
     sends = []
 
@@ -160,26 +158,20 @@
 
     @pl.when(is3)
     def _():
-        greet(row4, col4)
-        greet(row5, col4)
-
-    @pl.when(is4)
-    def _():
-        for step in range(4):
-            greet(row_group * 4 + step, col_of4)
-
-    @pl.when(is5)
-    def _():
-        for step in range(16):
-            greet(step, col_of5)
+        for apart in range(1, 16):
+            greet(lax.rem(row + apart, 16), col)
 
     order = reversed_digits(iota((TOK, TOK), 0)) == iota((TOK, TOK), 1)
     permute = onehot(order)
     permute_scaled = onehot(order, SCALE)
-    qp[...] = mm(permute_scaled, q_ref[...]).astype(BF16)
-    kp[...] = mm(permute, k_ref[...]).astype(BF16)
-    vp[...] = mm(permute, v_ref[...]).astype(BF16)
-    gp[...] = mm(permute, g_ref[...]).astype(BF16)
+    for load, table, src, dst in zip(
+        loads,
+        (permute_scaled, permute, permute, permute),
+        (q_in, g_in, k_in, v_in),
+        (qp, gp, kp, vp),
+    ):
+        load.wait()
+        dst[...] = mm(table, src[...]).astype(BF16)
 
     low64 = iota((64, LANES), 1) < HEAD_DIM
     low256 = iota((TOK, LANES), 1) < HEAD_DIM
@@ -197,13 +189,13 @@
                     one = swap(one)
                 pack[w, i, slot] = jnp.where(low64, one, two).astype(BF16)
 
-    pl.semaphore_wait(barrier, 15 + jnp.where(is3, 2, jnp.where(is4, 4, jnp.where(is5, 16, 0))))
+    pl.semaphore_wait(barrier, jnp.where(is3, 30, 15))
 
     for h in range(HEADS):
         w, i = h % 4, h // 4
         post(
             pack.at[w, i, :, pl.ds(16 * i, 16), :],
-            recv_l.at[:, pl.ds(pl.multiple_of(16 * col, 16), 16), :],
+            recv3.at[:, pl.ds(pl.multiple_of(16 * col, 16), 16), :],
             1, row, h, maybe_self=True,
         )
     my_rows = pl.ds(pl.multiple_of(64 * member, 64), 64)
@@ -236,23 +228,35 @@
         d_all[unit] = dprob
         return stat
 
-    lax.fori_loop(0, 3, pair_forward, 0)
+    lax.fori_loop(0, PAIRS, pair_forward, 0)
 
     @pl.when(is3)
     def _():
-        arrive(recv_l, 1)
+        arrive(recv3, 1)
         pick4 = onehot(
             iota((64, TOK), 1) == 16 * (iota((64, TOK), 0) >> 2) + (iota((64, TOK), 0) & 3)
         )
         pick5 = onehot(iota((16, TOK), 1) == 16 * iota((16, TOK), 0))
         for slot in range(2):
-            sel_c[slot] = mm(pick4, recv_l[slot]).astype(BF16)
-            sel_d[slot] = mm(pick5, recv_l[slot]).astype(BF16)
-
-    post(sel_c, recv_l.at[:, pl.ds(pl.multiple_of(64 * row_in, 64), 64), :], 1, row4, col4, cond=is3)
-    post(sel_d, recv_l.at[:, pl.ds(pl.multiple_of(16 * row, 16), 16), :], 1, row5, col4, cond=is3)
-
-    lax.fori_loop(3, PAIRS, pair_forward, 0)
+            sel4[slot] = mm(pick4, recv3[slot]).astype(BF16)
+            sel5[slot] = mm(pick5, recv3[slot]).astype(BF16)
+
+    rows4 = pl.ds(pl.multiple_of(64 * row_in, 64), 64)
+    rows5 = pl.ds(pl.multiple_of(16 * row, 16), 16)
+
+    def across(src, dst, count, recv):
+        for apart in range(1, count):
+            to_row = lax.rem(row + apart, 16) if count == 16 else (
+                row_group * 4 + lax.rem(row_in + apart, 4)
+            )
+            post(src, dst, recv, to_row, col, cond=is3)
+
+        @pl.when(is3)
+        def _():
+            pltpu.make_async_copy(src, dst, recv_sem.at[recv]).start()
+
+    across(sel5, recv5.at[:, rows5, :], 16, 7)
+    across(sel4, recv4.at[:, rows4, :], 4, 6)
 
     for h in range(HEADS):
         w, i = h % 4, h // 4
@@ -279,23 +283,14 @@
             c_two.at[member], 4, row, group * 4 + w, maybe_self=True,
         )
 
-    @pl.when(is45)
+
+    @pl.when(is3)
     def _():
-        arrive(recv_l, 1)
-
-    @pl.when(has_long)
-    def _():
-        st_l[...] = packed_forward(recv_l[0], recv_l[1], HEADS + 3)
-
-    for step in range(4):
-        post(
-            st_l.at[:, pl.ds(LANES * (step // 2), LANES)], e_four, 6,
-            row_group * 4 + step, col_of4, cond=is4,
-        )
-    for step in range(16):
-        post(
-            st_l.at[:, pl.ds(LANES * (step // 8), LANES)], f_five, 7, step, col_of5, cond=is5
-        )
+        st_l[0] = packed_forward(recv3[0], recv3[1], 15)
+        arrive(recv4, 6)
+        st_l[1] = packed_forward(recv4[0], recv4[1], 16)
+        arrive(recv5, 7)
+        st_l[2] = packed_forward(recv5[0], recv5[1], 17)
 
     lane = iota((1, TOK), 1)
     src128 = iota((LANES, TOK), 0)
@@ -323,33 +318,28 @@
             onehot(src256 == 64 * ((dst256 >> 4) & 3) + 16 * group + (dst256 & 15)),
         ).reshape(4, 8, TOK)
         two = rows_of(picked(two, 4, lambda c: (lane >> 6) == c))
-        arrive(e_four, 6)
         four = move(
-            e_four[...],
+            st_l[1],
             onehot(
                 jnp.logical_and(
-                    src128 == 64 * lax.rem(row_in, 2) + 4 * (dst128 >> 4) + (dst128 & 15),
-                    (dst128 & 15) < 4,
+                    src256 == 64 * row_in + 4 * (dst256 >> 4) + (dst256 & 15),
+                    (dst256 & 15) < 4,
                 )
             ),
         )
         four = masked_rows(four, (lane & 15) < 4)
-        arrive(f_five, 7)
         five = move(
-            f_five[...],
+            st_l[2],
             onehot(
-                jnp.logical_and(
-                    src128 == 16 * lax.rem(row, 8) + (dst128 >> 4), (dst128 & 15) == 0
-                )
+                jnp.logical_and(src256 == 16 * row + (dst256 >> 4), (dst256 & 15) == 0)
             ),
         )
         five = masked_rows(five, (lane & 15) == 0)
-        lse, delta = merge([one, two, rows_of(st_l[...]), four, five])
+        lse, delta = merge([one, two, rows_of(st_l[0]), four, five])
         st3[...] = stat_tile(lse, delta, 0.0)
-        fin_l[...] = stat_tile(lse, delta, 0.0)
-
-    post(st3, i_three.at[row_in], 10, row4, col4, cond=is3)
-    post(st3, j_three.at[row], 11, row5, col4, cond=is3)
+
+    across(st3, j_three.at[row], 16, 11)
+    across(st3, i_three.at[row_in], 4, 10)
     col_head = jnp.where(is3, col, 0)
     for step in range(4):
         post(
@@ -361,23 +351,6 @@
             st3.at[:, pl.ds(LANES * (step // 8), LANES)], g_three.at[col_head], 8,
             row, step, cond=is3, maybe_self=True,
         )
-
-    @pl.when(is4)
-    def _():
-        arrive(i_three, 10)
-        total = move(
-            i_three[...].reshape(4 * 8, TOK),
-            onehot(src256 == 16 * ((dst256 >> 2) & 15) + (dst256 & 3)),
-        ).reshape(4, 8, TOK)
-        fin_l[...] = picked(total, 4, lambda c: (lane >> 6) == c)
-
-    @pl.when(is5)
-    def _():
-        arrive(j_three, 11)
-        total = move(
-            j_three[...].reshape(16 * 8, TOK), onehot(src256 == 16 * (dst256 & 15))
-        ).reshape(16, 8, TOK)
-        fin_l[...] = picked(total, 16, lambda c: (lane >> 4) == c)
 
     def packed_backward(query_side, key_side, unit, stat, final):
         probs, dscore = backward(
@@ -388,20 +361,6 @@
             probs, jnp.where(low256, zero, query_side)
         )
         return both, mm_tn(dscore, jnp.where(low256, key_side, zero))
-
-    @pl.when(has_long)
-    def _():
-        both, own = packed_backward(recv_l[0], recv_l[1], HEADS + 3, st_l[...], fin_l[...])
-        out_l[0] = both.astype(BF16)
-        out_l[1] = own.astype(BF16)
-
-    for step in range(4):
-        post(
-            out_l.at[:, pl.ds(64 * step, 64), :], back4, 12,
-            row_group * 4 + step, col_of4, cond=is4,
-        )
-    for step in range(16):
-        post(out_l.at[:, pl.ds(16 * step, 16), :], back5, 13, step, col_of5, cond=is5)
 
     spread64 = onehot(src128 == 64 * lax.rem(member, 2) + (dst128 & 63))
     arrive(b_own, 3)
@@ -435,14 +394,34 @@
 
     @pl.when(is3)
     def _():
+        both3, own3 = packed_backward(recv3[0], recv3[1], 15, st_l[0], st3[...])
+        arrive(i_three, 10)
+        total = move(
+            i_three[...].reshape(4 * 8, TOK),
+            onehot(src256 == 16 * ((dst256 >> 2) & 15) + (dst256 & 3)),
+        ).reshape(4, 8, TOK)
+        total = picked(total, 4, lambda c: (lane >> 6) == c)
+        both4, own4 = packed_backward(recv4[0], recv4[1], 16, st_l[1], total)
+        part4[0] = both4
+        part4[1] = own4
+        arrive(j_three, 11)
+        total = move(
+            j_three[...].reshape(16 * 8, TOK), onehot(src256 == 16 * (dst256 & 15))
+        ).reshape(16, 8, TOK)
+        total = picked(total, 16, lambda c: (lane >> 4) == c)
+        both5, own5 = packed_backward(recv5[0], recv5[1], 17, st_l[2], total)
+        part5[0] = both5
+        part5[1] = own5
         place4 = onehot(
             iota((TOK, 64), 0) == 16 * (iota((TOK, 64), 1) >> 2) + (iota((TOK, 64), 1) & 3)
         )
         place5 = onehot(iota((TOK, 16), 0) == 16 * iota((TOK, 16), 1))
-        arrive(back4, 12)
-        arrive(back5, 13)
-        for slot in range(2):
-            total = out_l[slot].astype(F32) + mm(place4, back4[slot]) + mm(place5, back5[slot])
+        for slot, base in enumerate((both3, own3)):
+            total = (
+                base
+                + mm(place4, part4[slot, rows4, :].astype(BF16))
+                + mm(place5, part5[slot, rows5, :].astype(BF16))
+            )
             out_l[slot] = total.astype(BF16)
 
     for step in range(16):
@@ -513,9 +492,9 @@
             acc_q[rows, tile] += own
             acc_k[rows, tile] += grad_k
             acc_v[rows, tile] += grad_v
-    dq_ref[...] = mm(permute_scaled, acc_q[...].astype(BF16)).astype(BF16)
-    dk_ref[...] = mm(permute, acc_k[...].astype(BF16)).astype(BF16)
-    dv_ref[...] = mm(permute, acc_v[...].astype(BF16)).astype(BF16)
+    sum_q[...] = acc_q[...].astype(BF16)
+    sum_k[...] = acc_k[...].astype(BF16)
+    sum_v[...] = acc_v[...].astype(BF16)
 
     for away, copy in sends:
         if away is None:
@@ -524,56 +503,82 @@
             pl.when(away)(copy.wait_send)
 
 
+def restore(sum_q, sum_k, sum_v, dq_hbm, dk_hbm, dv_hbm, dq, dk, dv, sems):
+    order = reversed_digits(iota((TOK, TOK), 0)) == iota((TOK, TOK), 1)
+    copies = []
+    for slot, (src, tile, dst) in enumerate(
+        ((sum_q, dq, dq_hbm), (sum_k, dk, dk_hbm), (sum_v, dv, dv_hbm))
+    ):
+        table = onehot(order, SCALE if slot == 0 else 1.0)
+        tile[...] = mm(table, src[...]).astype(BF16)
+        copy = pltpu.make_async_copy(tile, dst, sems.at[slot])
+        copy.start()
+        copies.append(copy)
+    for copy in copies:
+        copy.wait()
+
+
 def body(queries, keys, values, grad_out):
-    def vm(shape, kind):
-        return pltpu.VMEM(shape, kind)
-
+    vm = pltpu.VMEM
     whole = pl.BlockSpec(memory_space=pltpu.VMEM)
-    return pl.pallas_call(
+    hbm = pl.BlockSpec(memory_space=pltpu.HBM)
+    array = jax.ShapeDtypeStruct((TOK, WIDTH), BF16)
+    queries, keys, values, grad_out = [
+        pltpu.with_memory_space_constraint(x, pltpu.HBM) for x in (queries, keys, values, grad_out)
+    ]
+    sums = pl.pallas_call(
         kernel,
-        out_shape=[jax.ShapeDtypeStruct((TOK, WIDTH), BF16)] * 3,
-        in_specs=[whole] * 4,
+        out_shape=[array] * 3,
+        in_specs=[hbm] * 4,
         out_specs=[whole] * 3,
-        scratch_shapes=[vm((TOK, WIDTH), BF16)] * 4
+        scratch_shapes=[vm((TOK, WIDTH), BF16)] * 8
         + [vm((TOK, WIDTH), F32)] * 3
         + [
-            vm((16, TOK, TOK), F32),
-            vm((16, TOK, TOK), F32),
+            vm((18, TOK, TOK), F32),
+            vm((18, TOK, TOK), F32),
             vm((4, 3, 2, 64, LANES), BF16),
             vm((3, 2, TOK, LANES), BF16),
+            vm((2, TOK, LANES), BF16),
+            vm((2, TOK, LANES), BF16),
             vm((2, TOK, LANES), BF16),
             vm((2, 64, LANES), BF16),
             vm((2, 16, LANES), BF16),
             vm((4, 3, 8, TOK), F32),
             vm((3, 8, TOK), F32),
-            vm((8, TOK), F32),
+            vm((3, 8, TOK), F32),
             vm((HEADS, 8, TOK), F32),
             vm((3, 8, TOK), F32),
-            vm((8, TOK), F32),
             vm((8, TOK), F32),
             vm((16, 8, LANES), F32),
             vm((4, 3, 8, LANES), F32),
             vm((4, 3, 8, LANES), F32),
             vm((4, 8, TOK), F32),
-            vm((8, LANES), F32),
-            vm((8, LANES), F32),
             vm((HEADS, 8, LANES), F32),
             vm((3, 8, LANES), F32),
             vm((4, 8, TOK), F32),
             vm((16, 8, TOK), F32),
             vm((3, 2, TOK, LANES), BF16),
             vm((2, TOK, LANES), BF16),
-            vm((2, 64, LANES), BF16),
-            vm((2, 16, LANES), BF16),
+            vm((2, TOK, LANES), F32),
+            vm((2, TOK, LANES), F32),
             vm((4, 3, 2, 64, LANES), BF16),
             vm((HEADS, 2, 16, LANES), BF16),
             pltpu.SemaphoreType.DMA((128,)),
             pltpu.SemaphoreType.DMA((16,)),
+            pltpu.SemaphoreType.DMA((4,)),
         ],
         compiler_params=pltpu.CompilerParams(
             collective_id=0, has_side_effects=True, vmem_limit_bytes=48 * 1024 * 1024
         ),
     )(queries, keys, values, grad_out)
+    return pl.pallas_call(
+        restore,
+        out_shape=[array] * 3,
+        in_specs=[whole] * 3,
+        out_specs=[hbm] * 3,
+        scratch_shapes=[vm((TOK, WIDTH), BF16)] * 3 + [pltpu.SemaphoreType.DMA((3,))],
+        compiler_params=pltpu.CompilerParams(vmem_limit_bytes=16 * 1024 * 1024),
+    )(*sums)
 
 
 def solution(mesh):

time: 57.8 us -> 39.8 us (0.69)
  Pallas kernels: 50.7 us -> 39.1 us
  local copies, waits for them, and re-layouts: 6.21 us -> 0 us
    pallas_call x1 -> x2, Pallas kernels: 50.7 us -> 39.1 us  [the longest x1 37.8 us: body(): pl.pallas_call(kernel, out_shape=[array] * 3, in_specs=[hbm] * 4, out_spe...]
    unnamed x11 -> x0, local copies, waits for them, and re-layouts: 6.21 us -> none
where the time goes in v1:
time: 39.8 us; the launch traced here: 39.7 us
  Pallas kernels  39.1 us (98%)
  between operations  0.64 us (2%)
    pallas_call x1, Pallas kernels, body(): pl.pallas_call(kernel, out_shape=[array] * 3, in_specs=[hbm] * 4, out_spe...  37.8 us
    pallas_call x1, Pallas kernels, body(): pl.pallas_call(restore, out_shape=[array] * 3, in_specs=[whole] * 3, out_...  1.32 us

profile of v1, /device:TPU:1, one launch (start us, length us, event | category | flops | bytes accessed | tf_op | source)
XLA Modules:
  0.0 39.7 jit_solution(1061113082389747812)
XLA Ops:
  0.6 37.8 %shard_map.67 = (bf16[256,768]{1,0:T(8,128)(2,1)S(1)}, bf16[256,768]{1,0:T(8,128)(2,1)S(1)}, bf16[256,768]{1,0:T(8,128)(2,1)S(1)}) custom-call(bf16[256,768]{1,0:T(8,128)(2,1)} %q_hbm.1, bf16[256,768]{1,0:T(8,128)(2,1)} %k_hbm.1, bf16[256,768]{1,0:T(8,128)(2,1)} %v_hbm.1, bf16[256,768]{1,0:T(8,128)(2,1)} %g_hbm.1), custom_call_target="tpu_custom_call" | custom-call | tf_op jit(solution)/shard_map/pallas_call | solution.py:529
  38.4 1.3 %shard_map.68 = (bf16[256,768]{1,0:T(8,128)(2,1)}, bf16[256,768]{1,0:T(8,128)(2,1)}, bf16[256,768]{1,0:T(8,128)(2,1)}) custom-call(bf16[256,768]{1,0:T(8,128)(2,1)S(1)} %get-tuple-element.6.sum_q, bf16[256,768]{1,0:T(8,128)(2,1)S(1)} %get-tuple-element.7.sum_k, bf16[256,768]{1,0:T(8,128)(2,1)S(1)} %get-tuple-element.8.sum_v), custom_call_target="tpu_custom_call" | custom-call | tf_op jit(solution)/shard_map/pallas_call | solution.py:574

commit v2 on v1

v2 whole, which is shorter than its diff:
```python
import jax
import jax.numpy as jnp
from jax import lax
from jax.experimental import pallas as pl
from jax.experimental.pallas import tpu as pltpu
from jax.sharding import PartitionSpec as P

HEADS = 12
HEAD_DIM = 64
TOK = 256
WIDTH = 768
LANES = 128
SCALE = HEAD_DIM**-0.5
NEG_FILL = -1e30
PAIRS = HEADS // 2
MESH = pl.DeviceIdType.MESH
FAR_FIRST = (8, 9, 7, 10, 6, 11, 5, 12, 4, 13, 3, 14, 2, 15, 1)
F32 = jnp.float32
BF16 = jnp.bfloat16


def mm(a, b):
    return lax.dot_general(a, b, (((1,), (0,)), ((), ())), preferred_element_type=F32)


def mm_nt(a, b):
    return lax.dot_general(a, b, (((1,), (1,)), ((), ())), preferred_element_type=F32)


def mm_tn(a, b):
    return lax.dot_general(a, b, (((0,), (0,)), ((), ())), preferred_element_type=F32)


def iota(shape, dim):
    return lax.broadcasted_iota(jnp.int32, shape, dim)


def onehot(hit, value=1.0):
    return jnp.where(hit, value, 0.0).astype(BF16)


def move(rows, table):
    count = rows.shape[0]
    high = rows.astype(BF16).astype(F32)
    rest = rows - high
    middle = rest.astype(BF16).astype(F32)
    parts = jnp.concatenate([high, middle, rest - middle], axis=0).astype(BF16)
    moved = mm(parts, table)
    return moved[:count] + moved[count : 2 * count] + moved[2 * count :]


def swap(tile):
    return pltpu.roll(tile, HEAD_DIM, 1)


def reversed_digits(index):
    return (index & 3) * 64 + ((index >> 2) & 3) * 16 + ((index >> 4) & 3) * 4 + (index >> 6)


def forward(scores, dprob):
    row_max = jnp.max(scores, axis=0, keepdims=True)
    weights = jnp.exp(scores - row_max)
    row_sum = jnp.sum(weights, axis=0, keepdims=True)
    dot_sum = jnp.sum(weights * dprob, axis=0, keepdims=True)
    return weights, stat_tile(row_max + jnp.log(row_sum), dot_sum / row_sum, row_max)


def stat_tile(lse, delta, row_max):
    row = iota((8, TOK), 0)
    return jnp.where(row == 0, lse, jnp.where(row == 1, delta, jnp.where(row == 2, row_max, 0.0)))


def backward(weights, dprob, row_max, lse, delta):
    probs = weights * jnp.exp(row_max - lse)
    dscore = probs * (dprob - delta)
    return probs.astype(BF16), dscore.astype(BF16)


def merge(parts):
    top = parts[0][0]
    for lse, _ in parts[1:]:
        top = jnp.maximum(top, lse)
    norm = 0.0
    total = 0.0
    for lse, delta in parts:
        factor = jnp.exp(lse - top)
        norm = norm + factor
        total = total + factor * delta
    return top + jnp.log(norm), total / norm


def rows_of(tile):
    return tile[0:1], tile[1:2]


def masked_rows(tile, hit):
    lse, delta = rows_of(tile)
    return jnp.where(hit, lse, NEG_FILL), jnp.where(hit, delta, 0.0)


def kernel(
    q_hbm, k_hbm, v_hbm, g_hbm, sum_q, sum_k, sum_v,
    q_in, k_in, v_in, g_in, qp, kp, vp, gp, acc_q, acc_k, acc_v,
    w_all, d_all, pack, recv_a, recv3, recv4, recv5, sel4, sel5,
    st1, st2, st_l, fin1, fin2, st3, st4_out, st5_out,
    a_own, b_own, c_two, d_two, g_three, h_three, i_three, j_three,
    tab_a, tab_d, tab_out, tab_64, tab_16, tab_h, tab_p4, tab_p5,
    out2, out_l, base3, keyed4, keyed5, back2, back3,
    send_sem, recv_sem, load_sem,
):
    row = lax.axis_index("row")
    col = lax.axis_index("col")
    member = lax.rem(col, 4)
    group = col // 4
    row_in = lax.rem(row, 4)
    row_group = row // 4
    is3 = col < HEADS

    loads = []
    for slot, (src, dst) in enumerate(
        ((q_hbm, q_in), (g_hbm, g_in), (k_hbm, k_in), (v_hbm, v_in))
    ):
        load = pltpu.make_async_copy(src, dst, load_sem.at[slot])
        load.start()
        loads.append(load)

    barrier = pltpu.get_barrier_semaphore()

    def greet(to_row, to_col):
        pl.semaphore_signal(barrier, inc=1, device_id=(to_row, to_col), device_id_type=MESH)

    @pl.when(is3)
    def _():
        for apart in FAR_FIRST:
            greet(lax.rem(row + apart, 16), col)

    for apart in range(1, 16):
        greet(row, lax.rem(col + apart, 16))

    slots = iter(range(144))
    sent_all, sent3, sent_not3 = [], [], []

    def remote(src, dst, recv, to_row, to_col, into, like=None):
        slot = next(slots)
        copy = pltpu.make_async_remote_copy(
            src_ref=src, dst_ref=dst, send_sem=send_sem.at[slot],
            recv_sem=recv_sem.at[recv], device_id=(to_row, to_col), device_id_type=MESH,
        )
        if like is None:
            into.append(copy.wait_send)
        else:
            into.append(lambda: pltpu.make_async_copy(like(), like(), send_sem.at[slot]).wait())
        return copy

    def local(src, dst, recv):
        pltpu.make_async_copy(src, dst, recv_sem.at[recv]).start()

    def arrive(buffer, recv):
        pltpu.make_async_copy(buffer, buffer, recv_sem.at[recv]).wait()

    def to_workers(source, dst, recv):
        base = jnp.where(is3, col, 3 * (col - HEADS))
        for apart in range(HEADS):
            h = lax.rem(base + apart, HEADS)
            src = source(h & 3, h >> 2)
            copy = remote(src, dst, recv, row, h, sent_all if apart else sent_not3)
            if apart:
                copy.start()
            else:
                pl.when(is3)(lambda: local(src, dst, recv))
                pl.when(jnp.logical_not(is3))(copy.start)

    def to_group(source, dst, recv):
        for apart in (2, 3, 1):
            w = lax.rem(member + apart, 4)
            remote(source(w), dst, recv, row, group * 4 + w, sent_all).start()
        local(source(member), dst, recv)

    def to_cols(targets, source, dst, recv):
        for to_col in targets:
            remote(source(to_col), dst, recv, row, to_col, sent3, lambda: source(0)).start()

    def to_rows(source, dst, recv, count):
        for apart in FAR_FIRST if count == 16 else (2, 3, 1):
            target = lax.rem(row + apart, 16) if count == 16 else (
                row_group * 4 + lax.rem(row_in + apart, 4)
            )
            remote(source(), dst, recv, target, col, sent3, source).start()
        local(source(), dst, recv)

    def lane_block(index):
        return pl.ds(pl.multiple_of(LANES * index, LANES), LANES)

    order = reversed_digits(iota((TOK, TOK), 0)) == iota((TOK, TOK), 1)
    permute = onehot(order)
    permute_scaled = onehot(order, SCALE)
    for load, table, src, dst in zip(
        loads,
        (permute_scaled, permute, permute, permute),
        (q_in, g_in, k_in, v_in),
        (qp, gp, kp, vp),
    ):
        load.wait()
        dst[...] = mm(table, src[...]).astype(BF16)

    low64 = iota((64, LANES), 1) < HEAD_DIM
    low256 = iota((TOK, LANES), 1) < HEAD_DIM

    for w in range(4):
        rows = slice(64 * w, 64 * w + 64)
        for i in range(3):
            tile = slice(LANES * (2 * i + w // 2), LANES * (2 * i + w // 2) + LANES)
            for slot, (first, second) in enumerate(((qp, gp), (kp, vp))):
                one = first[rows, tile].astype(F32)
                two = second[rows, tile].astype(F32)
                if w % 2 == 0:
                    two = swap(two)
                else:
                    one = swap(one)
                pack[w, i, slot] = jnp.where(low64, one, two).astype(BF16)

    pl.semaphore_wait(barrier, jnp.where(is3, 30, 15))

    to_workers(
        lambda w, i: pack.at[w, i, :, pl.ds(pl.multiple_of(16 * i, 16), 16), :],
        recv3.at[:, pl.ds(pl.multiple_of(16 * col, 16), 16), :], 1,
    )
    my_rows = pl.ds(pl.multiple_of(64 * member, 64), 64)
    to_group(lambda w: pack.at[w], recv_a.at[:, :, my_rows, :], 0)

    lane = iota((1, TOK), 1)
    src128 = iota((LANES, TOK), 0)
    dst128 = iota((LANES, TOK), 1)
    src256 = iota((TOK, TOK), 0)
    dst256 = iota((TOK, TOK), 1)
    both = jnp.logical_and
    start = 64 * lax.rem(member, 2) + 16 * group
    tab_a[...] = onehot(src128 == start + (dst128 & 15))
    tab_d[...] = onehot(src256 == 64 * ((dst256 >> 4) & 3) + 16 * group + (dst256 & 15))
    lane5 = both(src256 == 16 * (dst256 & 15), (dst256 >> 4) == lax.rem(row, 8))
    lane4 = both(
        src256 == 16 * ((dst256 >> 2) & 15) + (dst256 & 3),
        ((dst256 >> 6) & 1) == lax.rem(row_in, 2),
    )
    tab_out[...] = onehot(
        jnp.logical_or(both(lane5, dst256 < LANES), both(lane4, dst256 >= LANES))
    )
    tab_64[...] = onehot(src128 == 64 * lax.rem(member, 2) + (dst128 & 63))
    tab_16[...] = onehot(src128 == 16 * lax.rem(col, 8) + (dst128 & 15))
    tab_h[...] = onehot(
        src128 == 64 * lax.rem(group, 2) + 16 * (dst128 >> 6) + (dst128 & 15)
    )
    tab_p4[...] = onehot(
        iota((TOK, 64), 0) == 16 * (iota((TOK, 64), 1) >> 2) + (iota((TOK, 64), 1) & 3)
    )
    tab_p5[...] = onehot(iota((TOK, 16), 0) == 16 * iota((TOK, 16), 1))

    def pair_forward(j, carry):
        lanes = pl.ds(pl.multiple_of(j * LANES, LANES), LANES)
        q, k, v, g = qp[:, lanes], kp[:, lanes], vp[:, lanes], gp[:, lanes]
        zero = jnp.zeros_like(k)
        i = j // 2
        for parity in range(2):
            mine = low256 if parity == 0 else jnp.logical_not(low256)
            scores = mm_nt(jnp.where(mine, k, zero), q)
            dprob = mm_nt(jnp.where(mine, v, zero), g)
            weights, stat = forward(scores, dprob)
            w_all[2 * j + parity] = weights
            d_all[2 * j + parity] = dprob
            st1[2 * lax.rem(j, 2) + parity, i] = stat
        return carry

    def packed_forward(query_side, key_side, unit):
        zero = jnp.zeros_like(key_side)
        scores = mm_nt(jnp.where(low256, key_side, zero), query_side)
        dprob = mm_nt(jnp.where(low256, zero, key_side), query_side)
        weights, stat = forward(scores, dprob)
        w_all[unit] = weights
        d_all[unit] = dprob
        return stat

    lax.fori_loop(0, PAIRS, pair_forward, 0)

    rows4 = pl.ds(pl.multiple_of(64 * row_in, 64), 64)
    rows5 = pl.ds(pl.multiple_of(16 * row, 16), 16)

    @pl.when(is3)
    def _():
        pick4 = onehot(
            iota((64, TOK), 1) == 16 * (iota((64, TOK), 0) >> 2) + (iota((64, TOK), 0) & 3)
        )
        pick5 = onehot(iota((16, TOK), 1) == 16 * iota((16, TOK), 0))
        arrive(recv3, 1)
        sel5[1] = mm(pick5, recv3[1]).astype(BF16)
        sel4[1] = mm(pick4, recv3[1]).astype(BF16)
        to_rows(lambda: sel5.at[1], recv5.at[1, rows5, :], 7, 16)
        to_rows(lambda: sel4.at[1], recv4.at[1, rows4, :], 6, 4)
        sel5[0] = mm(pick5, recv3[0]).astype(BF16)
        sel4[0] = mm(pick4, recv3[0]).astype(BF16)

    to_workers(lambda w, i: st1.at[w, i, :, lane_block(w >> 1)], a_own.at[col], 2)
    to_group(lambda w: st1.at[w, :, :, lane_block(w >> 1)], b_own.at[member], 3)

    arrive(recv_a, 0)
    for i in range(3):
        st2[i] = packed_forward(recv_a[i, 0], recv_a[i, 1], HEADS + i)
    for apart in range(3):
        i = lax.rem(group + apart, 3)
        copy = remote(
            st2.at[i], d_two.at[group], 5, row, member + 4 * i, sent_all if apart else sent_not3
        )
        if apart:
            copy.start()
        else:
            pl.when(is3)(lambda: local(st2.at[group], d_two.at[group], 5))
            pl.when(jnp.logical_not(is3))(copy.start)
    to_group(lambda w: st2.at[:, :, lane_block(w >> 1)], c_two.at[member], 4)

    kept4 = (lane & 15) < 4
    kept5 = (lane & 15) == 0

    def picked(moved, count, hit):
        total = jnp.zeros((8, TOK), F32)
        for step in range(count):
            total = total + jnp.where(hit(step), moved[step], 0.0)
        return total

    @pl.when(is3)
    def _():
        to_rows(lambda: sel5.at[0], recv5.at[0, rows5, :], 13, 16)
        to_rows(lambda: sel4.at[0], recv4.at[0, rows4, :], 12, 4)

    @pl.when(is3)
    def _():
        st_l[0] = packed_forward(recv3[0], recv3[1], 15)
        arrive(a_own, 2)
        one = move(a_own[...].reshape(16 * 8, LANES), tab_a[...]).reshape(16, 8, TOK)
        one = rows_of(picked(one, 16, lambda c: (lane >> 4) == c))
        arrive(d_two, 5)
        two = move(d_two[...].reshape(4 * 8, TOK), tab_d[...]).reshape(4, 8, TOK)
        two = rows_of(picked(two, 4, lambda c: (lane >> 6) == c))
        early = merge([one, two, rows_of(st_l[0])])
        arrive(recv4.at[1], 6)
        st_l[1] = packed_forward(recv3[0], recv4[1], 16)
        arrive(recv5.at[1], 7)
        st_l[2] = packed_forward(recv3[0], recv5[1], 17)
        lse, delta = merge(
            [early, masked_rows(st_l[1], kept4), masked_rows(st_l[2], kept5)]
        )
        final = stat_tile(lse, delta, 0.0)
        st3[...] = final

        def block(to_col):
            return st3.at[:, lane_block(to_col >> 3)]

        to_cols(
            [4 * ((group + apart) & 3) + member for apart in range(1, 4)],
            block, h_three.at[group], 9,
        )
        local(block(col), h_three.at[group], 9)
        moved = move(final, tab_out[...])
        st5_out[...] = moved[0:2, :LANES]
        st4_out[...] = moved[0:2, LANES:]
        to_rows(lambda: st5_out, j_three.at[row], 11, 16)
        to_rows(lambda: st4_out, i_three.at[row_in], 10, 4)
        to_cols(
            [
                4 * ((group + apart) & 3) + ((member + beside) & 3)
                for beside in range(1, 4)
                for apart in range(4)
            ],
            block, g_three.at[member, group], 8,
        )

    def packed_backward(query_side, key_side, unit, stat, final):
        probs, dscore = backward(
            w_all[unit], d_all[unit], stat[2:3], final[0:1], final[1:2]
        )
        zero = jnp.zeros_like(key_side)
        both = mm(dscore, jnp.where(low256, query_side, zero)) + mm(
            probs, jnp.where(low256, zero, query_side)
        )
        return both, mm_tn(dscore, jnp.where(low256, key_side, zero))

    others_of_row = [lax.rem(col + apart, 16) for apart in range(1, 16)]

    def rows_of_owner(slot, to_col):
        return out_l.at[slot, pl.ds(pl.multiple_of(16 * to_col, 16), 16), :]

    def low_part(tile, low):
        return jnp.where(low, tile, jnp.zeros_like(tile))

    def high_part(tile, low):
        return jnp.where(low, jnp.zeros_like(tile), tile)

    @pl.when(is3)
    def _():
        pair3, own = packed_backward(recv3[0], recv3[1], 15, st_l[0], st3[...])
        base3[...] = pair3
        for unit, keys_of, kept in ((1, recv4, kept4), (2, recv5, kept5)):
            _, dscore = backward(
                w_all[15 + unit], d_all[15 + unit],
                jnp.where(kept, st_l[unit, 2:3], NEG_FILL), st3[0:1], st3[1:2],
            )
            own = own + mm_tn(dscore, low_part(keys_of[1], low256))
        out_l[1] = own.astype(BF16)
        to_cols(others_of_row, lambda to_col: rows_of_owner(1, to_col), back3.at[col, 1], 16)
        local(rows_of_owner(1, col), back3.at[col, 1], 16)
        arrive(recv4.at[0], 12)
        arrive(recv5.at[0], 13)
        for keyed, own_rows, others in ((keyed4, sel4, recv4), (keyed5, sel5, recv5)):
            low = iota(own_rows.shape[1:], 1) < HEAD_DIM
            keyed[0] = mm_nt(low_part(own_rows[1], low), others[0])
            keyed[1] = mm_nt(high_part(own_rows[1], low), others[0])

    arrive(b_own, 3)
    arrive(h_three, 9)
    local(h_three, g_three.at[member], 8)
    own2 = move(b_own[...].reshape(4 * 3 * 8, LANES), tab_64[...]).reshape(4, 3, 8, TOK)
    long2 = move(h_three[...].reshape(3 * 8, LANES), tab_h[...]).reshape(3, 8, TOK)
    for i in range(3):
        one = rows_of(picked(own2[:, i], 4, lambda c: (lane >> 6) == c))
        lse, delta = merge([one, rows_of(st2[i])])
        long = ((lane >> 4) & 3) == i
        fin2[i] = stat_tile(
            jnp.where(long, long2[i][0:1], lse), jnp.where(long, long2[i][1:2], delta), 0.0
        )

    swapped = []
    for i in range(3):
        pair, own = packed_backward(recv_a[i, 0], recv_a[i, 1], HEADS + i, st2[i], fin2[i])
        out2[i] = pair.astype(BF16)
        swapped.append(own)
    out2[3] = (swapped[0] + swap(swapped[1])).astype(BF16)
    out2[4] = swapped[2].astype(BF16)
    to_group(
        lambda w: out2.at[:, pl.ds(pl.multiple_of(64 * w, 64), 64), :], back2.at[member], 14
    )

    @pl.when(is3)
    def _():
        def keyed_backward(keyed, total, others):
            probs = jnp.exp(keyed[0] - total[0:1])
            dscore = probs * (keyed[1] - total[1:2])
            pair = mm(dscore.astype(BF16), low_part(others[0], low256)) + mm(
                probs.astype(BF16), high_part(others[0], low256)
            )
            return pair.astype(BF16)

        arrive(i_three, 10)
        total = jnp.concatenate([i_three[0] + i_three[1], i_three[2] + i_three[3]], axis=1)
        pair = base3[...] + mm(tab_p4[...], keyed_backward(keyed4, total, recv4))
        arrive(j_three, 11)
        halves = []
        for half in range(2):
            some = j_three[8 * half]
            for step in range(1, 8):
                some = some + j_three[8 * half + step]
            halves.append(some)
        total = jnp.concatenate(halves, axis=1)
        pair = pair + mm(tab_p5[...], keyed_backward(keyed5, total, recv5))
        out_l[0] = pair.astype(BF16)

        to_cols(others_of_row, lambda to_col: rows_of_owner(0, to_col), back3.at[col, 0], 15)
        local(rows_of_owner(0, col), back3.at[col, 0], 15)

    arrive(c_two, 4)
    arrive(g_three, 8)
    two1 = move(c_two[...].reshape(HEADS * 8, LANES), tab_64[...]).reshape(4, 3, 8, TOK)
    three1 = move(g_three[...].reshape(HEADS * 8, LANES), tab_16[...]).reshape(4, 3, 8, TOK)
    for h in range(HEADS):
        w, i = h % 4, h // 4
        one = rows_of(st1[w, i])
        lse, delta = merge([one, masked_rows(two1[w, i], (lane >> 6) == w)])
        long = (lane >> 4) == 4 * w + i
        fin1[h] = stat_tile(
            jnp.where(long, three1[w, i][0:1], lse), jnp.where(long, three1[w, i][1:2], delta), 0.0
        )

    def pair_backward(j, carry):
        lanes = pl.ds(pl.multiple_of(j * LANES, LANES), LANES)
        q, k, g = qp[:, lanes], kp[:, lanes], gp[:, lanes]
        zero = jnp.zeros_like(k)
        i = j // 2
        sum_q = sum_k = sum_v = 0.0
        for parity in range(2):
            mine = low256 if parity == 0 else jnp.logical_not(low256)
            h = 2 * j + parity
            stat = st1[2 * lax.rem(j, 2) + parity, i]
            final = fin1[h]
            probs, dscore = backward(w_all[h], d_all[h], stat[2:3], final[0:1], final[1:2])
            sum_v = sum_v + mm(probs, jnp.where(mine, g, zero))
            sum_k = sum_k + mm(dscore, jnp.where(mine, q, zero))
            sum_q = sum_q + mm_tn(dscore, jnp.where(mine, k, zero))
        acc_q[:, lanes] = sum_q
        acc_k[:, lanes] = sum_k
        acc_v[:, lanes] = sum_v
        return carry

    lax.fori_loop(0, PAIRS, pair_backward, 0)

    for left in sent_all:
        left()

    @pl.when(is3)
    def _():
        for left in sent3:
            left()

    @pl.when(jnp.logical_not(is3))
    def _():
        for left in sent_not3:
            left()

    def returned(w, count, pair, own, own_low):
        low = iota((count, LANES), 1) < HEAD_DIM
        pair = pair.astype(F32)
        own = own.astype(F32)
        other = swap(pair)
        if (w % 2 == 0) != own_low:
            own = swap(own)
        if w % 2 == 0:
            return [jnp.where(low, part, 0.0) for part in (own, pair, other)]
        return [jnp.where(low, 0.0, part) for part in (own, other, pair)]

    heads = [
        (h, h % 4, h // 4, slice(LANES * (h // 2), LANES * (h // 2) + LANES))
        for h in range(HEADS)
    ]
    sums = ((acc_q, sum_q), (acc_k, sum_k), (acc_v, sum_v))
    arrive(back2, 14)
    for h, w, i, tile in heads:
        rows = slice(64 * w, 64 * w + 64)
        parts = returned(w, 64, back2[w, i], back2[w, 3 + i // 2], i != 1)
        for part, (acc, _) in zip(parts, sums):
            acc[rows, tile] += part
    for acc, out in sums:
        out[...] = acc[...].astype(BF16)
    arrive(back3.at[:, 1], 16)
    arrive(back3.at[:, 0], 15)
    for h, w, i, tile in heads:
        rows = slice(64 * w + 16 * i, 64 * w + 16 * i + 16)
        parts = returned(w, 16, back3[h, 0], back3[h, 1], True)
        for part, (acc, out) in zip(parts, sums):
            out[rows, tile] = (acc[rows, tile] + part).astype(BF16)


def restore(sum_q, sum_k, sum_v, dq_hbm, dk_hbm, dv_hbm, dq, dk, dv, sems):
    order = reversed_digits(iota((TOK, TOK), 0)) == iota((TOK, TOK), 1)
    copies = []
    for slot, (src, tile, dst) in enumerate(
        ((sum_q, dq, dq_hbm), (sum_k, dk, dk_hbm), (sum_v, dv, dv_hbm))
    ):
        table = onehot(order, SCALE if slot == 0 else 1.0)
        tile[...] = mm(table, src[...]).astype(BF16)
        copy = pltpu.make_async_copy(tile, dst, sems.at[slot])
        copy.start()
        copies.append(copy)
    for copy in copies:
        copy.wait()


def body(queries, keys, values, grad_out):
    vm = pltpu.VMEM
    whole = pl.BlockSpec(memory_space=pltpu.VMEM)
    hbm = pl.BlockSpec(memory_space=pltpu.HBM)
    array = jax.ShapeDtypeStruct((TOK, WIDTH), BF16)
    queries, keys, values, grad_out = [
        pltpu.with_memory_space_constraint(x, pltpu.HBM) for x in (queries, keys, values, grad_out)
    ]
    sums = pl.pallas_call(
        kernel,
        out_shape=[array] * 3,
        in_specs=[hbm] * 4,
        out_specs=[whole] * 3,
        scratch_shapes=[vm((TOK, WIDTH), BF16)] * 8
        + [vm((TOK, WIDTH), F32)] * 3
        + [
            vm((18, TOK, TOK), F32),
            vm((18, TOK, TOK), F32),
            vm((4, 3, 2, 64, LANES), BF16),
            vm((3, 2, TOK, LANES), BF16),
            vm((2, TOK, LANES), BF16),
            vm((2, TOK, LANES), BF16),
            vm((2, TOK, LANES), BF16),
            vm((2, 64, LANES), BF16),
            vm((2, 16, LANES), BF16),
            vm((4, 3, 8, TOK), F32),
            vm((3, 8, TOK), F32),
            vm((3, 8, TOK), F32),
            vm((HEADS, 8, TOK), F32),
            vm((3, 8, TOK), F32),
            vm((8, TOK), F32),
            vm((2, LANES), F32),
            vm((2, LANES), F32),
            vm((16, 8, LANES), F32),
            vm((4, 3, 8, LANES), F32),
            vm((4, 3, 8, LANES), F32),
            vm((4, 8, TOK), F32),
            vm((4, 3, 8, LANES), F32),
            vm((3, 8, LANES), F32),
            vm((4, 2, LANES), F32),
            vm((16, 2, LANES), F32),
            vm((LANES, TOK), BF16),
            vm((TOK, TOK), BF16),
            vm((TOK, TOK), BF16),
            vm((LANES, TOK), BF16),
            vm((LANES, TOK), BF16),
            vm((LANES, TOK), BF16),
            vm((TOK, 64), BF16),
            vm((TOK, 16), BF16),
            vm((5, TOK, LANES), BF16),
            vm((2, TOK, LANES), BF16),
            vm((TOK, LANES), F32),
            vm((2, 64, TOK), F32),
            vm((2, 16, TOK), F32),
            vm((4, 5, 64, LANES), BF16),
            vm((HEADS, 2, 16, LANES), BF16),
            pltpu.SemaphoreType.DMA((144,)),
            pltpu.SemaphoreType.DMA((17,)),
            pltpu.SemaphoreType.DMA((4,)),
        ],
        compiler_params=pltpu.CompilerParams(
            collective_id=0, has_side_effects=True, vmem_limit_bytes=48 * 1024 * 1024
        ),
    )(queries, keys, values, grad_out)
    return pl.pallas_call(
        restore,
        out_shape=[array] * 3,
        in_specs=[whole] * 3,
        out_specs=[hbm] * 3,
        scratch_shapes=[vm((TOK, WIDTH), BF16)] * 3 + [pltpu.SemaphoreType.DMA((3,))],
        compiler_params=pltpu.CompilerParams(vmem_limit_bytes=16 * 1024 * 1024),
    )(*sums)


def solution(mesh):
    spec = P(("row", "col"), None)
    return jax.shard_map(
        body, mesh=mesh, in_specs=(spec,) * 4, out_specs=(spec,) * 3, check_vma=False
    )
```

time: 39.8 us -> 38.7 us (0.972)
  Pallas kernels: 39.1 us -> 37.9 us
    pallas_call x1, Pallas kernels: 37.8 us -> 36.6 us  [body(): pl.pallas_call(kernel, out_shape=[array] * 3, in_specs=[hbm] * 4, out_spe...]
where the time goes in v2:
time: 38.7 us; the launch traced here: 38.6 us
  Pallas kernels  37.9 us (98%)
  between operations  0.64 us (2%)
    pallas_call x1, Pallas kernels, body(): pl.pallas_call(kernel, out_shape=[array] * 3, in_specs=[hbm] * 4, out_spe...  36.6 us
    pallas_call x1, Pallas kernels, body(): pl.pallas_call(restore, out_shape=[array] * 3, in_specs=[whole] * 3, out_...  1.32 us

profile of v2, /device:TPU:1, one launch (start us, length us, event | category | flops | bytes accessed | tf_op | source)
XLA Modules:
  0.0 38.6 jit_solution(12755385945439562445)
XLA Ops:
  0.6 36.6 %shard_map.67 = (bf16[256,768]{1,0:T(8,128)(2,1)S(1)}, bf16[256,768]{1,0:T(8,128)(2,1)S(1)}, bf16[256,768]{1,0:T(8,128)(2,1)S(1)}) custom-call(bf16[256,768]{1,0:T(8,128)(2,1)} %q_hbm.1, bf16[256,768]{1,0:T(8,128)(2,1)} %k_hbm.1, bf16[256,768]{1,0:T(8,128)(2,1)} %v_hbm.1, bf16[256,768]{1,0:T(8,128)(2,1)} %g_hbm.1), custom_call_target="tpu_custom_call" | custom-call | tf_op jit(solution)/shard_map/pallas_call | solution.py:571
  37.2 1.3 %shard_map.68 = (bf16[256,768]{1,0:T(8,128)(2,1)}, bf16[256,768]{1,0:T(8,128)(2,1)}, bf16[256,768]{1,0:T(8,128)(2,1)}) custom-call(bf16[256,768]{1,0:T(8,128)(2,1)S(1)} %get-tuple-element.6.sum_q, bf16[256,768]{1,0:T(8,128)(2,1)S(1)} %get-tuple-element.7.sum_k, bf16[256,768]{1,0:T(8,128)(2,1)S(1)} %get-tuple-element.8.sum_v), custom_call_target="tpu_custom_call" | custom-call | tf_op jit(solution)/shard_map/pallas_call | solution.py:627

commit v3 on v2

--- a/solution.py
+++ b/solution.py
@@ -99,7 +99,7 @@
 
 
 def kernel(
-    q_hbm, k_hbm, v_hbm, g_hbm, sum_q, sum_k, sum_v,
+    q_hbm, k_hbm, v_hbm, g_hbm, sum_q, sum_k, sum_v, order_out,
     q_in, k_in, v_in, g_in, qp, kp, vp, gp, acc_q, acc_k, acc_v,
     w_all, d_all, pack, recv_a, recv3, recv4, recv5, sel4, sel5,
     st1, st2, st_l, fin1, fin2, st3, st4_out, st5_out,
@@ -194,6 +194,7 @@
     order = reversed_digits(iota((TOK, TOK), 0)) == iota((TOK, TOK), 1)
     permute = onehot(order)
     permute_scaled = onehot(order, SCALE)
+    order_out[...] = permute
     for load, table, src, dst in zip(
         loads,
         (permute_scaled, permute, permute, permute),
@@ -334,15 +335,15 @@
     def _():
         st_l[0] = packed_forward(recv3[0], recv3[1], 15)
         arrive(a_own, 2)
+        arrive(d_two, 5)
         one = move(a_own[...].reshape(16 * 8, LANES), tab_a[...]).reshape(16, 8, TOK)
         one = rows_of(picked(one, 16, lambda c: (lane >> 4) == c))
-        arrive(d_two, 5)
         two = move(d_two[...].reshape(4 * 8, TOK), tab_d[...]).reshape(4, 8, TOK)
         two = rows_of(picked(two, 4, lambda c: (lane >> 6) == c))
         early = merge([one, two, rows_of(st_l[0])])
         arrive(recv4.at[1], 6)
+        arrive(recv5.at[1], 7)
         st_l[1] = packed_forward(recv3[0], recv4[1], 16)
-        arrive(recv5.at[1], 7)
         st_l[2] = packed_forward(recv3[0], recv5[1], 17)
         lse, delta = merge(
             [early, masked_rows(st_l[1], kept4), masked_rows(st_l[2], kept5)]
@@ -353,16 +354,16 @@
         def block(to_col):
             return st3.at[:, lane_block(to_col >> 3)]
 
-        to_cols(
-            [4 * ((group + apart) & 3) + member for apart in range(1, 4)],
-            block, h_three.at[group], 9,
-        )
-        local(block(col), h_three.at[group], 9)
         moved = move(final, tab_out[...])
         st5_out[...] = moved[0:2, :LANES]
         st4_out[...] = moved[0:2, LANES:]
         to_rows(lambda: st5_out, j_three.at[row], 11, 16)
         to_rows(lambda: st4_out, i_three.at[row_in], 10, 4)
+        to_cols(
+            [4 * ((group + apart) & 3) + member for apart in range(1, 4)],
+            block, h_three.at[group], 9,
+        )
+        local(block(col), h_three.at[group], 9)
         to_cols(
             [
                 4 * ((group + apart) & 3) + ((member + beside) & 3)
@@ -433,10 +434,6 @@
         swapped.append(own)
     out2[3] = (swapped[0] + swap(swapped[1])).astype(BF16)
     out2[4] = swapped[2].astype(BF16)
-    to_group(
-        lambda w: out2.at[:, pl.ds(pl.multiple_of(64 * w, 64), 64), :], back2.at[member], 14
-    )
-
     @pl.when(is3)
     def _():
         def keyed_backward(keyed, total, others):
@@ -448,21 +445,24 @@
             return pair.astype(BF16)
 
         arrive(i_three, 10)
-        total = jnp.concatenate([i_three[0] + i_three[1], i_three[2] + i_three[3]], axis=1)
-        pair = base3[...] + mm(tab_p4[...], keyed_backward(keyed4, total, recv4))
         arrive(j_three, 11)
-        halves = []
-        for half in range(2):
-            some = j_three[8 * half]
-            for step in range(1, 8):
-                some = some + j_three[8 * half + step]
-            halves.append(some)
-        total = jnp.concatenate(halves, axis=1)
-        pair = pair + mm(tab_p5[...], keyed_backward(keyed5, total, recv5))
+        total4 = jnp.concatenate([i_three[0] + i_three[1], i_three[2] + i_three[3]], axis=1)
+        total5 = jnp.concatenate(
+            [jnp.sum(j_three[0:8], axis=0), jnp.sum(j_three[8:16], axis=0)], axis=1
+        )
+        pair = (
+            base3[...]
+            + mm(tab_p4[...], keyed_backward(keyed4, total4, recv4))
+            + mm(tab_p5[...], keyed_backward(keyed5, total5, recv5))
+        )
         out_l[0] = pair.astype(BF16)
 
         to_cols(others_of_row, lambda to_col: rows_of_owner(0, to_col), back3.at[col, 0], 15)
         local(rows_of_owner(0, col), back3.at[col, 0], 15)
+
+    to_group(
+        lambda w: out2.at[:, pl.ds(pl.multiple_of(64 * w, 64), 64), :], back2.at[member], 14
+    )
 
     arrive(c_two, 4)
     arrive(g_three, 8)
@@ -534,25 +534,23 @@
         parts = returned(w, 64, back2[w, i], back2[w, 3 + i // 2], i != 1)
         for part, (acc, _) in zip(parts, sums):
             acc[rows, tile] += part
-    for acc, out in sums:
-        out[...] = acc[...].astype(BF16)
+    for (acc, out), factor in zip(sums, (SCALE, 1.0, 1.0)):
+        out[...] = (acc[...] * factor).astype(BF16)
     arrive(back3.at[:, 1], 16)
     arrive(back3.at[:, 0], 15)
     for h, w, i, tile in heads:
         rows = slice(64 * w + 16 * i, 64 * w + 16 * i + 16)
         parts = returned(w, 16, back3[h, 0], back3[h, 1], True)
-        for part, (acc, out) in zip(parts, sums):
-            out[rows, tile] = (acc[rows, tile] + part).astype(BF16)
-
-
-def restore(sum_q, sum_k, sum_v, dq_hbm, dk_hbm, dv_hbm, dq, dk, dv, sems):
-    order = reversed_digits(iota((TOK, TOK), 0)) == iota((TOK, TOK), 1)
+        for part, (acc, out), factor in zip(parts, sums, (SCALE, 1.0, 1.0)):
+            out[rows, tile] = ((acc[rows, tile] + part) * factor).astype(BF16)
+
+
+def restore(sum_q, sum_k, sum_v, order, dq_hbm, dk_hbm, dv_hbm, dq, dk, dv, sems):
     copies = []
     for slot, (src, tile, dst) in enumerate(
         ((sum_q, dq, dq_hbm), (sum_k, dk, dk_hbm), (sum_v, dv, dv_hbm))
     ):
-        table = onehot(order, SCALE if slot == 0 else 1.0)
-        tile[...] = mm(table, src[...]).astype(BF16)
+        tile[...] = mm(order[...], src[...]).astype(BF16)
         copy = pltpu.make_async_copy(tile, dst, sems.at[slot])
         copy.start()
         copies.append(copy)
@@ -570,9 +568,9 @@
     ]
     sums = pl.pallas_call(
         kernel,
-        out_shape=[array] * 3,
+        out_shape=[array] * 3 + [jax.ShapeDtypeStruct((TOK, TOK), BF16)],
         in_specs=[hbm] * 4,
-        out_specs=[whole] * 3,
+        out_specs=[whole] * 4,
         scratch_shapes=[vm((TOK, WIDTH), BF16)] * 8
         + [vm((TOK, WIDTH), F32)] * 3
         + [
@@ -627,7 +625,7 @@
     return pl.pallas_call(
         restore,
         out_shape=[array] * 3,
-        in_specs=[whole] * 3,
+        in_specs=[whole] * 4,
         out_specs=[hbm] * 3,
         scratch_shapes=[vm((TOK, WIDTH), BF16)] * 3 + [pltpu.SemaphoreType.DMA((3,))],
         compiler_params=pltpu.CompilerParams(vmem_limit_bytes=16 * 1024 * 1024),

time: 38.7 us -> 36.9 us (0.953)
  Pallas kernels: 37.9 us -> 36.2 us
    pallas_call x2, Pallas kernels: 37.9 us -> 36.2 us  [the longest x1 34.9 us: body(): pl.pallas_call(kernel, out_shape=[array] * 3 + [jax.ShapeDtypeStruct((TOK...]
where the time goes in v3:
time: 36.9 us; the launch traced here: 36.8 us
  Pallas kernels  36.2 us (98%)
  between operations  0.64 us (2%)
    pallas_call x1, Pallas kernels, body(): pl.pallas_call(kernel, out_shape=[array] * 3 + [jax.ShapeDtypeStruct((TOK...  34.9 us
    pallas_call x1, Pallas kernels, body(): pl.pallas_call(restore, out_shape=[array] * 3, in_specs=[whole] * 4, out_...  1.32 us

profile of v3, /device:TPU:1, one launch (start us, length us, event | category | flops | bytes accessed | tf_op | source)
XLA Modules:
  0.0 36.8 jit_solution(9716058142543618511)
XLA Ops:
  0.6 34.9 %shard_map.67 = (bf16[256,768]{1,0:T(8,128)(2,1)S(1)}, bf16[256,768]{1,0:T(8,128)(2,1)S(1)}, bf16[256,768]{1,0:T(8,128)(2,1)S(1)}, bf16[256,256]{1,0:T(8,128)(2,1)S(1)}) custom-call(bf16[256,768]{1,0:T(8,128)(2,1)} %q_hbm.1, bf16[256,768]{1,0:T(8,128)(2,1)} %k_hbm.1, bf16[256,768]{1,0:T(8,128)(2,1)} %v_hbm.1, bf16[256,768]{1,0:T(8,128)(2,1)} %g_hbm.1), custom_call_target="tpu_custom_call" | custom-call | tf_op jit(solution)/shard_map/pallas_call | solution.py:569
  35.5 1.3 %shard_map.68 = (bf16[256,768]{1,0:T(8,128)(2,1)}, bf16[256,768]{1,0:T(8,128)(2,1)}, bf16[256,768]{1,0:T(8,128)(2,1)}) custom-call(bf16[256,768]{1,0:T(8,128)(2,1)S(1)} %get-tuple-element.7.sum_q, bf16[256,768]{1,0:T(8,128)(2,1)S(1)} %get-tuple-element.8.sum_k, bf16[256,768]{1,0:T(8,128)(2,1)S(1)} %get-tuple-element.9.sum_v, ...), custom_call_target="tpu_custom_call" | custom-call | tf_op jit(solution)/shard_map/pallas_call | solution.py:625

commit v4 on v3

--- a/solution.py
+++ b/solution.py
@@ -137,7 +137,7 @@
     for apart in range(1, 16):
         greet(row, lax.rem(col + apart, 16))
 
-    slots = iter(range(144))
+    slots = iter(range(160))
     sent_all, sent3, sent_not3 = [], [], []
 
     def remote(src, dst, recv, to_row, to_col, into, like=None):
@@ -434,6 +434,11 @@
         swapped.append(own)
     out2[3] = (swapped[0] + swap(swapped[1])).astype(BF16)
     out2[4] = swapped[2].astype(BF16)
+    to_group(
+        lambda w: out2.at[3:5, pl.ds(pl.multiple_of(64 * w, 64), 64), :],
+        back2.at[member, 3:5], 14,
+    )
+
     @pl.when(is3)
     def _():
         def keyed_backward(keyed, total, others):
@@ -461,7 +466,8 @@
         local(rows_of_owner(0, col), back3.at[col, 0], 15)
 
     to_group(
-        lambda w: out2.at[:, pl.ds(pl.multiple_of(64 * w, 64), 64), :], back2.at[member], 14
+        lambda w: out2.at[0:3, pl.ds(pl.multiple_of(64 * w, 64), 64), :],
+        back2.at[member, 0:3], 14,
     )
 
     arrive(c_two, 4)
@@ -614,7 +620,7 @@
             vm((2, 16, TOK), F32),
             vm((4, 5, 64, LANES), BF16),
             vm((HEADS, 2, 16, LANES), BF16),
-            pltpu.SemaphoreType.DMA((144,)),
+            pltpu.SemaphoreType.DMA((160,)),
             pltpu.SemaphoreType.DMA((17,)),
             pltpu.SemaphoreType.DMA((4,)),
         ],

time: 36.9 us -> 36.9 us (level)
  no operation moved by 1% of the time
where the time goes in v4:
time: 36.9 us; the launch traced here: 36.8 us
  Pallas kernels  36.2 us (98%)
  between operations  0.64 us (2%)
    pallas_call x1, Pallas kernels, body(): pl.pallas_call(kernel, out_shape=[array] * 3 + [jax.ShapeDtypeStruct((TOK...  34.8 us
    pallas_call x1, Pallas kernels, body(): pl.pallas_call(restore, out_shape=[array] * 3, in_specs=[whole] * 4, out_...  1.32 us

profile of v4, /device:TPU:1, one launch (start us, length us, event | category | flops | bytes accessed | tf_op | source)
XLA Modules:
  0.0 36.8 jit_solution(7043326710105619867)
XLA Ops:
  0.6 34.8 %shard_map.67 = (bf16[256,768]{1,0:T(8,128)(2,1)S(1)}, bf16[256,768]{1,0:T(8,128)(2,1)S(1)}, bf16[256,768]{1,0:T(8,128)(2,1)S(1)}, bf16[256,256]{1,0:T(8,128)(2,1)S(1)}) custom-call(bf16[256,768]{1,0:T(8,128)(2,1)} %q_hbm.1, bf16[256,768]{1,0:T(8,128)(2,1)} %k_hbm.1, bf16[256,768]{1,0:T(8,128)(2,1)} %v_hbm.1, bf16[256,768]{1,0:T(8,128)(2,1)} %g_hbm.1), custom_call_target="tpu_custom_call" | custom-call | tf_op jit(solution)/shard_map/pallas_call | solution.py:575
  35.5 1.3 %shard_map.68 = (bf16[256,768]{1,0:T(8,128)(2,1)}, bf16[256,768]{1,0:T(8,128)(2,1)}, bf16[256,768]{1,0:T(8,128)(2,1)}) custom-call(bf16[256,768]{1,0:T(8,128)(2,1)S(1)} %get-tuple-element.7.sum_q, bf16[256,768]{1,0:T(8,128)(2,1)S(1)} %get-tuple-element.8.sum_k, bf16[256,768]{1,0:T(8,128)(2,1)S(1)} %get-tuple-element.9.sum_v, ...), custom_call_target="tpu_custom_call" | custom-call | tf_op jit(solution)/shard_map/pallas_call | solution.py:631
